TPU v7x, 256 devices: a whole 4x4x8 slice. The times are simulated.
256 devices in a mesh: tgt: 64 (over x, z, core), rep: 4 (over y).
Axes of the slice: x: 4, y: 4, z: 8, core: 2. Of those that a mesh axis runs over, the one named last changes fastest.
Arguments:
- flux: bfloat16 [16384, 7808], P(('tgt', 'rep')), may hold values from 0.19921875 to 4
- ivar: bfloat16 [16384, 7808], P(('tgt', 'rep')), may hold values from 0.099609375 to 10
- row_target: int32 [16384], P(('tgt', 'rep')), may hold values from 0 to 8191, as said below
- start_w: float32 [8192, 64], P(('tgt', 'rep')), may hold values from 0.02 to 0.25
- start_h: float32 [64, 7808], P(None, 'tgt'), may hold values from 0.02 to 0.25
Outputs:
- activations: float32 [8192, 64], P(('tgt', 'rep'))
- templates: float32 [64, 7808], P(None, 'tgt')
Inputs may be any that keep to these rules, and one draw needn't show every extreme that they name: `row_target`: row i lies on device d = i // 64; its target t is owned by device t // 32, which has the same index along rep as d, i.e. (t // 32) % 4 == d % 4. The rows of one device name targets of one owning device at most 2 times, and every device reaches 2 for some owner. A target may have several rows or none.
All inputs are finite; a program needn't handle non-finite values.
Results may differ from a plain program's by a relative error of at most 0.035.
Values may be sent and summed in bfloat16 or wider, within the bound.
No kernel may reach another device: no remote copies, remote signals or barrier semaphores. Data moves between devices by JAX's collectives and lax.ppermute only.
A program may use at most 64 MiB of HBM per device.

v0:
```python
import jax
import jax.numpy as jnp
from jax import lax
from jax.sharding import PartitionSpec as P

SWEEPS = 2
PRIOR_IVAR = 0.5
EPSILON = 1e-06


def update_columns(activation, cross, gram):

    def column_step(index, current):
        gram_col = lax.dynamic_index_in_dim(gram, index, 1, keepdims=False)
        pivot = lax.dynamic_index_in_dim(gram_col, index, 0, keepdims=False)
        column = lax.dynamic_index_in_dim(current, index, 1, keepdims=False)
        wanted = lax.dynamic_index_in_dim(cross, index, 1, keepdims=False)
        fitted = jnp.dot(current, gram_col, precision=lax.Precision.HIGHEST)
        updated = jnp.maximum(column + (wanted - fitted) / (pivot + EPSILON), 0.0)
        return lax.dynamic_update_index_in_dim(current, updated, index, 1)

    return lax.fori_loop(0, activation.shape[1], column_step, activation)


def update_rows(templates, proj, gram):

    def row_step(index, current):
        gram_row = lax.dynamic_index_in_dim(gram, index, 0, keepdims=False)
        pivot = lax.dynamic_index_in_dim(gram_row, index, 0, keepdims=False)
        row_now = lax.dynamic_index_in_dim(current, index, 0, keepdims=False)
        wanted = lax.dynamic_index_in_dim(proj, index, 0, keepdims=False)
        fitted = jnp.dot(gram_row, current, precision=lax.Precision.HIGHEST)
        updated = jnp.maximum(row_now + (wanted - fitted) / (pivot + EPSILON), 0.0)
        return lax.dynamic_update_index_in_dim(current, updated, index, 0)

    return lax.fori_loop(0, templates.shape[0], row_step, templates)


def shards(flux, ivar, row_target, start_w, start_h):
    tgt_count = lax.axis_size("tgt")
    rep_count = lax.axis_size("rep")
    rows_dev = flux.shape[0]
    tgt_dev = start_w.shape[0]
    weighted = (ivar.astype(jnp.float32) * flux.astype(jnp.float32)).astype(jnp.bfloat16)
    owner_dev = row_target // tgt_dev
    peer_dev = owner_dev // rep_count
    capacity = 2 * rows_dev // tgt_count
    peer_onehot = (peer_dev[:, None] == jnp.arange(tgt_count, dtype=jnp.int32)[None, :]).astype(
        jnp.int32
    )
    running = jnp.cumsum(peer_onehot, axis=0)
    slot_index = jnp.sum(running * peer_onehot, axis=1) - 1
    place = peer_dev * capacity + slot_index
    source_row = (
        jnp.zeros((tgt_count * capacity,), jnp.int32)
        .at[place]
        .set(jnp.arange(rows_dev, dtype=jnp.int32))
    )
    filled = jnp.zeros((tgt_count * capacity,), jnp.int32).at[place].set(1)
    keep_rows = filled[:, None].astype(jnp.bfloat16)
    send_weighted = jnp.take(weighted, source_row, axis=0) * keep_rows
    send_ivar = jnp.take(ivar, source_row, axis=0) * keep_rows
    send_target = jnp.where(filled == 1, jnp.take(row_target, source_row, axis=0), -1)
    got_weighted, got_ivar, got_target = (
        lax.all_to_all(send_weighted, "tgt", split_axis=0, concat_axis=0, tiled=True),
        lax.all_to_all(send_ivar, "tgt", split_axis=0, concat_axis=0, tiled=True),
        lax.all_to_all(send_target, "tgt", split_axis=0, concat_axis=0, tiled=True),
    )
    first_target = (lax.axis_index("tgt") * rep_count + lax.axis_index("rep")) * tgt_dev
    selector = (
        got_target[None, :] - first_target == jnp.arange(tgt_dev, dtype=jnp.int32)[:, None]
    ).astype(jnp.bfloat16)
    numerator = jnp.dot(selector, got_weighted, preferred_element_type=jnp.float32)
    denominator = jnp.dot(selector, got_ivar, preferred_element_type=jnp.float32)
    coadd = (numerator / (denominator + PRIOR_IVAR)).astype(jnp.bfloat16)
    spectra = lax.all_to_all(coadd, "tgt", split_axis=1, concat_axis=0, tiled=True)
    activation = lax.all_gather(start_w, "tgt", axis=0, tiled=True)
    templates = start_h
    for sweep in range(SWEEPS):
        templ_bf = templates.astype(jnp.bfloat16)
        hgram_part = jnp.dot(templates, templates.T, precision=lax.Precision.HIGHEST)
        cross_part = jnp.dot(spectra, templ_bf.T, preferred_element_type=jnp.float32)
        cross, hgram = lax.psum((cross_part, hgram_part), "tgt")
        activation = update_columns(activation, cross, hgram)
        proj_part = lax.dot_general(
            activation.astype(jnp.bfloat16),
            spectra,
            (((0,), (0,)), ((), ())),
            preferred_element_type=jnp.float32,
        )
        wgram_part = jnp.dot(activation.T, activation, precision=lax.Precision.HIGHEST)
        proj, wgram = lax.psum((proj_part, wgram_part), "rep")
        templates = update_rows(templates, proj, wgram)
    own_w = lax.dynamic_slice_in_dim(activation, lax.axis_index("tgt") * tgt_dev, tgt_dev, 0)
    return (own_w, templates)


def solution(mesh):
    placed = (
        P(("tgt", "rep"), None),
        P(("tgt", "rep"), None),
        P(("tgt", "rep")),
        P(("tgt", "rep"), None),
        P(None, "tgt"),
    )
    return jax.shard_map(
        shards,
        mesh=mesh,
        in_specs=placed,
        out_specs=(P(("tgt", "rep"), None), P(None, "tgt")),
        check_vma=False,
    )
```

profile of v0, /device:TPU:8, one launch (start us, length us, event | category | flops | bytes accessed | tf_op | source)
XLA Modules:
  0.0 1318.5 jit_solution(9789575537605206230)
XLA Ops:
  10.4 1.6 gather_fusion
  13.6 11.9 all-to-all-start
  25.6 6.4 gather_fusion.2
  32.2 3.1 gather_fusion.1
  35.3 4.0 select_multiply_fusion.1
  39.4 1.7 all_to_all.41
  41.1 10.3 all-to-all-start.2
  51.4 5.0 all_to_all.38
  56.4 44.1 %all-to-all-done.2 = bf16[64,2,7808]{2,1,0:T(2,128)(2,1)S(1)} async-done(((bf16[64,2,7808]{2,1,0:T(2,128)(2,1)}), bf16[64,2,7808]{2,1,0:T(2,128)(2,1)S(1)}, u32[]{:S(2)}, u32[]{:S(2)}) %all-to-all-start.2) | async-done | bytes 1998880 | tf_op jit(solution)/shard_map/all_to_all | solution.py:66
  100.5 6.3 all-to-all-start.1
  107.1 4.3 all_to_all.43
  111.7 43.9 %all-to-all-done.1 = bf16[64,2,7808]{2,1,0:T(2,128)(2,1)} async-done(((bf16[64,2,7808]{2,1,0:T(2,128)(2,1)}), bf16[64,2,7808]{2,1,0:T(2,128)(2,1)}, u32[]{:S(2)}, u32[]{:S(2)}) %all-to-all-start.1) | async-done | bytes 1998880 | tf_op jit(solution)/shard_map/all_to_all | solution.py:65
  155.6 4.3 all_to_all.40
  160.3 2.1 all_to_all.44
  162.5 1.1 copy.17
  163.6 5.9 all-to-all-start.3
  169.5 17.1 %all-to-all-done.3 = bf16[32,64,122]{2,0,1:T(8,128)(2,1)S(1)} async-done(((bf16[32,64,122]{2,0,1:T(8,128)(2,1)}), bf16[32,64,122]{2,0,1:T(8,128)(2,1)S(1)}, u32[]{:S(2)}, u32[]{:S(2)}) %all-to-all-start.3) | async-done | bytes 499744 | tf_op jit(solution)/shard_map/all_to_all | solution.py:76
  186.7 1.1 fusion.28
  188.0 247.9 %psum.57 = f32[64,64]{1,0:T(8,128)S(1)} all-reduce(f32[64,64]{1,0:T(8,128)S(1)} %fusion.36), channel_id=1, replica_groups=mesh['tgt'=64,'rep'=4] {'tgt'}, use_global_device_ids=true, to_apply=%region_0.1 | all-reduce | flops 4096 | bytes 32768 | tf_op jit(solution)/shard_map/psum | solution.py:83
  436.0 47.2 %all_gather.3 = f32[2048,64]{1,0:T(8,128)S(1)} all-gather(f32[32,64]{1,0:T(8,128)S(1)} %copy-done.4), channel_id=1, replica_groups=mesh['tgt'=64,'rep'=4] {'tgt'}, dimensions={0}, use_global_device_ids=true | all-gather | bytes 532480 | tf_op jit(solution)/shard_map/all_gather | solution.py:77
  483.5 181.6 %while.64 = (s32[]{:T(128)}, f32[2048,64]{0,1:T(8,128)S(1)}, f32[2048,64]{0,1:T(8,128)}, f32[64,64]{0,1:T(8,128)S(1)}, s32[]{:T(128)}, /*index=5*/s32[]{:T(128)}, s32[]{:T(128)}, f32[1,1]{0,1:T(1,128)}) while((s32[]{:T(128)}, f32[2048,64]{0,1:T(8,128)S(1)}, f32[2048,64]{0,1:T(8,128)}, f32[64,64]{0,1:T(8,128)S(1)}, s32[]{:T(128)}, ...), condition=%wide.region_7.9_spmd, body=%wide.region_6.8_spmd.sunk | while | flops 1581060 | bytes 615053 | solution.py:22
  483.5 0.9 constant_dynamic-slice_fusion.20
  486.4 0.9 constant_dynamic-slice_fusion.20
  497.7 0.9 constant_dynamic-slice_fusion.20
  500.6 0.9 constant_dynamic-slice_fusion.20
  503.4 0.9 constant_dynamic-slice_fusion.20
  506.2 0.9 constant_dynamic-slice_fusion.20
  509.1 0.9 constant_dynamic-slice_fusion.20
  511.9 0.9 constant_dynamic-slice_fusion.20
  514.8 0.9 constant_dynamic-slice_fusion.20
  523.3 0.9 constant_dynamic-slice_fusion.20
  526.1 0.9 constant_dynamic-slice_fusion.20
  528.9 0.9 constant_dynamic-slice_fusion.20
  531.8 0.9 constant_dynamic-slice_fusion.20
  534.6 0.9 constant_dynamic-slice_fusion.20
  537.4 0.9 constant_dynamic-slice_fusion.20
  540.3 0.9 constant_dynamic-slice_fusion.20
  551.6 0.9 constant_dynamic-slice_fusion.20
  554.5 0.9 constant_dynamic-slice_fusion.20
  560.1 0.9 constant_dynamic-slice_fusion.20
  565.8 0.9 constant_dynamic-slice_fusion.20
  568.7 0.9 constant_dynamic-slice_fusion.20
  571.5 0.9 constant_dynamic-slice_fusion.20
  574.3 0.9 constant_dynamic-slice_fusion.20
  577.2 0.9 constant_dynamic-slice_fusion.20
  580.0 0.9 constant_dynamic-slice_fusion.20
  591.3 0.9 constant_dynamic-slice_fusion.20
  594.2 0.9 constant_dynamic-slice_fusion.20
  597.0 0.9 constant_dynamic-slice_fusion.20
  599.9 0.9 constant_dynamic-slice_fusion.20
  602.7 0.9 constant_dynamic-slice_fusion.20
  605.5 0.9 constant_dynamic-slice_fusion.20
  608.4 0.9 constant_dynamic-slice_fusion.20
  616.9 0.9 constant_dynamic-slice_fusion.20
  619.7 0.9 constant_dynamic-slice_fusion.20
  622.6 0.9 constant_dynamic-slice_fusion.20
  625.4 0.9 constant_dynamic-slice_fusion.20
  665.9 14.8 %all-reduce.1 = (f32[64,122]{1,0:T(8,128)S(1)}, f32[64,64]{1,0:T(8,128)S(1)}) all-reduce(f32[64,122]{1,0:T(8,128)S(1)} %fusion.23, f32[64,64]{1,0:T(8,128)S(1)} %fusion.37), channel_id=1, replica_groups=mesh['tgt'=64,'rep'=4] {'rep'}, use_global_device_ids=true, to_apply=%region_9.11 | all-reduce | flops 11904 | bytes 95232 | tf_op jit(solution)/shard_map/psum | solution.py:92
  680.7 91.4 %while.65 = (s32[]{:T(128)}, f32[64,122]{1,0:T(8,128)S(1)}, f32[64,122]{1,0:T(8,128)S(1)}, f32[64,64]{1,0:T(8,128)S(1)}, s32[]{:T(128)}, /*index=5*/s32[]{:T(128)}, s32[]{:T(128)}, f32[1,1]{1,0:T(1,128)}) while((s32[]{:T(128)}, f32[64,122]{1,0:T(8,128)S(1)}, f32[64,122]{1,0:T(8,128)S(1)}, f32[64,64]{1,0:T(8,128)S(1)}, s32[]{:T(128)}, ...), condition=%wide.region_11.13_spmd, body=%wide.region_10.12_spmd.sunk | while | flops 94188 | bytes 37433 | solution.py:36
  772.2 1.1 fusion.26
  773.5 246.2 %psum.61 = f32[64,64]{1,0:T(8,128)S(1)} all-reduce(f32[64,64]{1,0:T(8,128)S(1)} %fusion.38), channel_id=1, replica_groups=mesh['tgt'=64,'rep'=4] {'tgt'}, use_global_device_ids=true, to_apply=%region_12.14 | all-reduce | flops 4096 | bytes 32768 | tf_op jit(solution)/shard_map/psum | solution.py:83
  1019.7 181.6 %while.66 = (s32[]{:T(128)}, f32[2048,64]{0,1:T(8,128)S(1)}, f32[2048,64]{0,1:T(8,128)}, f32[64,64]{0,1:T(8,128)S(1)}, s32[]{:T(128)}, /*index=5*/s32[]{:T(128)}, s32[]{:T(128)}, f32[1,1]{0,1:T(1,128)}) while((s32[]{:T(128)}, f32[2048,64]{0,1:T(8,128)S(1)}, f32[2048,64]{0,1:T(8,128)}, f32[64,64]{0,1:T(8,128)S(1)}, s32[]{:T(128)}, ...), condition=%wide.region_15.17_spmd, body=%wide.region_14.16_spmd.sunk | while | flops 1581060 | bytes 615053 | solution.py:22
  1202.4 17.2 %all-reduce = (f32[64,122]{1,0:T(8,128)S(1)}, f32[64,64]{1,0:T(8,128)S(1)}) all-reduce(f32[64,122]{1,0:T(8,128)S(1)} %fusion.21, f32[64,64]{1,0:T(8,128)S(1)} %fusion.39), channel_id=1, replica_groups=mesh['tgt'=64,'rep'=4] {'rep'}, use_global_device_ids=true, to_apply=%region_17.19 | all-reduce | flops 11904 | bytes 95232 | tf_op jit(solution)/shard_map/psum | solution.py:92
  1219.7 91.4 %while.67 = (s32[]{:T(128)}, f32[64,122]{1,0:T(8,128)S(1)}, f32[64,122]{1,0:T(8,128)S(1)}, f32[64,64]{1,0:T(8,128)S(1)}, s32[]{:T(128)}, /*index=5*/s32[]{:T(128)}, s32[]{:T(128)}, f32[1,1]{1,0:T(1,128)}) while((s32[]{:T(128)}, f32[64,122]{1,0:T(8,128)S(1)}, f32[64,122]{1,0:T(8,128)S(1)}, f32[64,64]{1,0:T(8,128)S(1)}, s32[]{:T(128)}, ...), condition=%wide.region_19.21_spmd, body=%wide.region_18.20_spmd.sunk | while | flops 94188 | bytes 37433 | solution.py:36
  (1035 shorter events, 345.4 us)
Async XLA Ops:
  13.6 27.5 %all-to-all-start = ((s32[64,2,1]{1,2,0:T(1,128)}), s32[64,2,1]{1,2,0:T(1,128)S(1)}, u32[]{:S(2)}, u32[]{:S(2)}) async-start(s32[64,2,1]{1,2,0:T(1,128)} %bitcast.26), calls=%async_computation | async-start | bytes 65536 | tf_op jit(solution)/shard_map/all_to_all | solution.py:67
  25.5 6.4 copy-start
  25.5 6.4 copy-start.3
  41.1 59.4 %all-to-all-start.2 = ((bf16[64,2,7808]{2,1,0:T(2,128)(2,1)}), bf16[64,2,7808]{2,1,0:T(2,128)(2,1)S(1)}, u32[]{:S(2)}, u32[]{:S(2)}) async-start(bf16[64,2,7808]{2,1,0:T(2,128)(2,1)} %all_to_all.41), calls=%async_computation.2 | async-start | bytes 3997696 | tf_op jit(solution)/shard_map/all_to_all | solution.py:66
  100.5 6.3 copy-start.2
  100.5 55.1 %all-to-all-start.1 = ((bf16[64,2,7808]{2,1,0:T(2,128)(2,1)}), bf16[64,2,7808]{2,1,0:T(2,128)(2,1)}, u32[]{:S(2)}, u32[]{:S(2)}) async-start(bf16[64,2,7808]{2,1,0:T(2,128)(2,1)} %all_to_all.38), calls=%async_computation.1 | async-start | bytes 3997696 | tf_op jit(solution)/shard_map/all_to_all | solution.py:65
  162.4 273.6 %copy-start.4 = (f32[32,64]{1,0:T(8,128)S(1)}, f32[32,64]{1,0:T(8,128)}, u32[]{:S(2)}) copy-start(f32[32,64]{1,0:T(8,128)} %param.18) | copy-start | bytes 24580
  163.6 23.1 %all-to-all-start.3 = ((bf16[32,64,122]{2,0,1:T(8,128)(2,1)}), bf16[32,64,122]{2,0,1:T(8,128)(2,1)S(1)}, u32[]{:S(2)}, u32[]{:S(2)}) async-start(bf16[32,64,122]{2,0,1:T(8,128)(2,1)} %copy.17), calls=%async_computation.3 | async-start | bytes 1048576 | tf_op jit(solution)/shard_map/all_to_all | solution.py:76
  169.5 314.1 %all-reduce.5.cloned.1.call-start = ((), (), s32[]{:S(2)}) async-start(), calls=%async_computation.4 | async-start | bytes 1048576 | tf_op jit(solution)/shard_map/psum | solution.py:83
  187.8 831.9 %all-reduce.7.cloned.1.call-start = ((), (), s32[]{:S(2)}) async-start(), calls=%async_computation.5 | async-start | bytes 1048576 | tf_op jit(solution)/shard_map/psum | solution.py:83
  1311.1 0.6 copy-start.1
Sparse Core Ops, SparseCore 0:
  187.9 178.6 all-reduce.4
  773.4 179.9 all-reduce.6
where the time goes:
time: 1330 us; the launch traced here: 1320 us
  blocking collectives  573 us (43%)
  local copies, waits for them, and re-layouts  335 us (25%)
  loops' own time  179 us (13%)
  waiting for transfers between devices  105 us (8%)
  matrix products  70.2 us (5%)
  starting transfers between devices  34.5 us (3%)
  between operations  14.4 us (1%)
    psum x2, blocking collectives, shards(): cross, hgram = lax.psum((cross_part, hgram_part), 'tgt')  494 us
    dynamic_slice x128, local copies, waits for them, and re-layouts, column_step(): wanted = lax.dynamic_index_in_dim(cross, index, 1, keepdims=False)  110 us
    another operation x2, loops' own time, update_columns(): return lax.fori_loop(0, activation.shape[1], column_step, activation)  93.4 us
    dynamic_slice x128, local copies, waits for them, and re-layouts, column_step(): pivot = lax.dynamic_index_in_dim(gram_col, index, 0, keepdims=False)  85.8 us
    another operation x2, loops' own time, update_rows(): return lax.fori_loop(0, templates.shape[0], row_step, templates)  85.8 us
    dynamic_slice x128, local copies, waits for them, and re-layouts, row_step(): pivot = lax.dynamic_index_in_dim(gram_row, index, 0, keepdims=False)  75.3 us
    all_gather x1, blocking collectives, shards(): activation = lax.all_gather(start_w, 'tgt', axis=0, tiled=True)  47.2 us
    dot_general x128, matrix products, column_step(): fitted = jnp.dot(current, gram_col, precision=lax.Precision.HIGHEST)  46.8 us
  transfers between devices with their start and end apart: 6, of which 3 were waited for; matrix products, arithmetic and copies ran while one was open for 1% of the time, Pallas kernels for 0%

commit v1 on v0

--- a/solution.py
+++ b/solution.py
@@ -74,7 +74,8 @@
     denominator = jnp.dot(selector, got_ivar, preferred_element_type=jnp.float32)
     coadd = (numerator / (denominator + PRIOR_IVAR)).astype(jnp.bfloat16)
     spectra = lax.all_to_all(coadd, "tgt", split_axis=1, concat_axis=0, tiled=True)
-    activation = lax.all_gather(start_w, "tgt", axis=0, tiled=True)
+    sent = jnp.stack([start_w] * lax.axis_size("tgt"))
+    activation = jnp.concatenate(lax.all_to_all(sent, "tgt", 0, 0), axis=0)
     templates = start_h
     for sweep in range(SWEEPS):
         templ_bf = templates.astype(jnp.bfloat16)

time: 1330 us -> 1290 us (0.970)
  blocking collectives: 573 us -> 530 us
    all_gather x1 -> x0, blocking collectives: 47.2 us -> none  [shards(): activation = lax.all_gather(start_w, 'tgt', axis=0, tiled=True)]
  transfers between devices with their start and end apart: 6 -> 7, of which waited for: 3 -> 3; matrix products, arithmetic and copies ran while one was open for 1% -> 2% of each run, Pallas kernels for 0% -> 0%
where the time goes in v1:
time: 1290 us; the launch traced here: 1280 us
  blocking collectives  530 us (41%)
  local copies, waits for them, and re-layouts  333 us (26%)
  loops' own time  176 us (14%)
  waiting for transfers between devices  104 us (8%)
  matrix products  71 us (6%)
  starting transfers between devices  40.9 us (3%)
  between operations  14.4 us (1%)
    psum x2, blocking collectives, shards(): cross, hgram = lax.psum((cross_part, hgram_part), 'tgt')  498 us
    dynamic_slice x128, local copies, waits for them, and re-layouts, column_step(): wanted = lax.dynamic_index_in_dim(cross, index, 1, keepdims=False)  110 us
    another operation x2, loops' own time, update_columns(): return lax.fori_loop(0, activation.shape[1], column_step, activation)  90.5 us
    another operation x2, loops' own time, update_rows(): return lax.fori_loop(0, templates.shape[0], row_step, templates)  85.8 us
    dynamic_slice x128, local copies, waits for them, and re-layouts, column_step(): pivot = lax.dynamic_index_in_dim(gram_col, index, 0, keepdims=False)  80.6 us
    dynamic_slice x128, local copies, waits for them, and re-layouts, row_step(): pivot = lax.dynamic_index_in_dim(gram_row, index, 0, keepdims=False)  75.3 us
    dot_general x128, matrix products, column_step(): fitted = jnp.dot(current, gram_col, precision=lax.Precision.HIGHEST)  46.8 us
    all_to_all x1, waiting for transfers between devices, shards(): lax.all_to_all(send_ivar, 'tgt', split_axis=0, concat_axis=0, tiled=True)  44.1 us
  transfers between devices with their start and end apart: 7, of which 3 were waited for; matrix products, arithmetic and copies ran while one was open for 2% of the time, Pallas kernels for 0%

profile of v1, /device:TPU:8, one launch (start us, length us, event | category | flops | bytes accessed | tf_op | source)
XLA Modules:
  0.0 1278.3 jit_solution(6263167141733972987)
XLA Ops:
  10.4 1.6 gather_fusion
  13.6 11.9 all-to-all-start.1
  25.6 6.4 gather_fusion.2
  32.2 3.1 gather_fusion.1
  35.3 4.0 select_multiply_fusion.1
  39.4 1.7 all_to_all.45
  41.1 10.3 all-to-all-start.3
  51.4 5.0 all_to_all.42
  56.4 44.1 %all-to-all-done.3 = bf16[64,2,7808]{2,1,0:T(2,128)(2,1)S(1)} async-done(((bf16[64,2,7808]{2,1,0:T(2,128)(2,1)}), bf16[64,2,7808]{2,1,0:T(2,128)(2,1)S(1)}, u32[]{:S(2)}, u32[]{:S(2)}) %all-to-all-start.3) | async-done | bytes 1998880 | tf_op jit(solution)/shard_map/all_to_all | solution.py:66
  100.5 6.3 all-to-all-start.2
  107.1 4.3 all_to_all.47
  111.7 43.9 %all-to-all-done.2 = bf16[64,2,7808]{2,1,0:T(2,128)(2,1)} async-done(((bf16[64,2,7808]{2,1,0:T(2,128)(2,1)}), bf16[64,2,7808]{2,1,0:T(2,128)(2,1)}, u32[]{:S(2)}, u32[]{:S(2)}) %all-to-all-start.2) | async-done | bytes 1998880 | tf_op jit(solution)/shard_map/all_to_all | solution.py:65
  155.6 4.3 all_to_all.44
  159.9 1.2 fusion.20
  161.1 3.2 all_to_all.48
  164.3 1.2 copy.22
  165.4 5.9 all-to-all-start.4
  171.4 1.4 reshape.124
  172.9 15.6 %all-to-all-done.4 = bf16[32,64,122]{2,0,1:T(8,128)(2,1)S(1)} async-done(((bf16[32,64,122]{2,0,1:T(8,128)(2,1)}), bf16[32,64,122]{2,0,1:T(8,128)(2,1)S(1)}, u32[]{:S(2)}, u32[]{:S(2)}) %all-to-all-start.4) | async-done | bytes 499744 | tf_op jit(solution)/shard_map/all_to_all | solution.py:76
  188.5 6.4 all-to-all-start
  195.0 1.1 fusion.28
  196.4 251.8 %psum.57 = f32[64,64]{1,0:T(8,128)S(1)} all-reduce(f32[64,64]{1,0:T(8,128)S(1)} %fusion.36), channel_id=1, replica_groups=mesh['tgt'=64,'rep'=4] {'tgt'}, use_global_device_ids=true, to_apply=%region_0.1 | all-reduce | flops 4096 | bytes 32768 | tf_op jit(solution)/shard_map/psum | solution.py:84
  448.8 1.9 reduce.4
  451.5 173.5 %while.64 = (s32[]{:T(128)}, f32[2048,64]{0,1:T(8,128)S(1)}, f32[2048,64]{0,1:T(8,128)}, f32[64,64]{0,1:T(8,128)S(1)}, s32[]{:T(128)}, /*index=5*/s32[]{:T(128)}, s32[]{:T(128)}, f32[1,1]{0,1:T(1,128)}) while((s32[]{:T(128)}, f32[2048,64]{0,1:T(8,128)S(1)}, f32[2048,64]{0,1:T(8,128)}, f32[64,64]{0,1:T(8,128)S(1)}, s32[]{:T(128)}, ...), condition=%wide.region_7.9_spmd, body=%wide.region_6.8_spmd.sunk | while | flops 1581060 | bytes 615053 | solution.py:22
  454.2 0.9 constant_dynamic-slice_fusion.20
  456.9 0.9 constant_dynamic-slice_fusion.20
  462.3 0.9 constant_dynamic-slice_fusion.20
  465.0 0.9 constant_dynamic-slice_fusion.20
  470.4 0.9 constant_dynamic-slice_fusion.20
  473.1 0.9 constant_dynamic-slice_fusion.20
  475.9 0.9 constant_dynamic-slice_fusion.20
  478.6 0.9 constant_dynamic-slice_fusion.20
  481.3 0.9 constant_dynamic-slice_fusion.20
  484.0 0.9 constant_dynamic-slice_fusion.20
  489.4 0.9 constant_dynamic-slice_fusion.20
  492.1 0.9 constant_dynamic-slice_fusion.20
  497.5 0.9 constant_dynamic-slice_fusion.20
  500.3 0.9 constant_dynamic-slice_fusion.20
  505.7 0.9 constant_dynamic-slice_fusion.20
  508.4 0.9 constant_dynamic-slice_fusion.20
  513.8 0.9 constant_dynamic-slice_fusion.20
  516.5 0.9 constant_dynamic-slice_fusion.20
  519.2 0.9 constant_dynamic-slice_fusion.20
  521.9 0.9 constant_dynamic-slice_fusion.20
  524.7 0.9 constant_dynamic-slice_fusion.20
  530.1 0.9 constant_dynamic-slice_fusion.20
  532.8 0.9 constant_dynamic-slice_fusion.20
  538.2 0.9 constant_dynamic-slice_fusion.20
  543.6 0.9 constant_dynamic-slice_fusion.20
  546.3 0.9 constant_dynamic-slice_fusion.20
  551.8 0.9 constant_dynamic-slice_fusion.20
  554.5 0.9 constant_dynamic-slice_fusion.20
  557.2 0.9 constant_dynamic-slice_fusion.20
  559.9 0.9 constant_dynamic-slice_fusion.20
  562.6 0.9 constant_dynamic-slice_fusion.20
  565.3 0.9 constant_dynamic-slice_fusion.20
  570.7 0.9 constant_dynamic-slice_fusion.20
  625.7 14.8 %all-reduce.1 = (f32[64,122]{1,0:T(8,128)S(1)}, f32[64,64]{1,0:T(8,128)S(1)}) all-reduce(f32[64,122]{1,0:T(8,128)S(1)} %fusion.23, f32[64,64]{1,0:T(8,128)S(1)} %fusion.37), channel_id=1, replica_groups=mesh['tgt'=64,'rep'=4] {'rep'}, use_global_device_ids=true, to_apply=%region_9.11 | all-reduce | flops 11904 | bytes 95232 | tf_op jit(solution)/shard_map/psum | solution.py:93
  640.6 91.4 %while.65 = (s32[]{:T(128)}, f32[64,122]{1,0:T(8,128)S(1)}, f32[64,122]{1,0:T(8,128)S(1)}, f32[64,64]{1,0:T(8,128)S(1)}, s32[]{:T(128)}, /*index=5*/s32[]{:T(128)}, s32[]{:T(128)}, f32[1,1]{1,0:T(1,128)}) while((s32[]{:T(128)}, f32[64,122]{1,0:T(8,128)S(1)}, f32[64,122]{1,0:T(8,128)S(1)}, f32[64,64]{1,0:T(8,128)S(1)}, s32[]{:T(128)}, ...), condition=%wide.region_11.13_spmd, body=%wide.region_10.12_spmd.sunk | while | flops 94188 | bytes 37433 | solution.py:36
  732.0 1.1 fusion.26
  733.3 246.3 %psum.61 = f32[64,64]{1,0:T(8,128)S(1)} all-reduce(f32[64,64]{1,0:T(8,128)S(1)} %fusion.38), channel_id=1, replica_groups=mesh['tgt'=64,'rep'=4] {'tgt'}, use_global_device_ids=true, to_apply=%region_12.14 | all-reduce | flops 4096 | bytes 32768 | tf_op jit(solution)/shard_map/psum | solution.py:84
  979.7 181.6 %while.66 = (s32[]{:T(128)}, f32[2048,64]{0,1:T(8,128)S(1)}, f32[2048,64]{0,1:T(8,128)}, f32[64,64]{0,1:T(8,128)S(1)}, s32[]{:T(128)}, /*index=5*/s32[]{:T(128)}, s32[]{:T(128)}, f32[1,1]{0,1:T(1,128)}) while((s32[]{:T(128)}, f32[2048,64]{0,1:T(8,128)S(1)}, f32[2048,64]{0,1:T(8,128)}, f32[64,64]{0,1:T(8,128)S(1)}, s32[]{:T(128)}, ...), condition=%wide.region_15.17_spmd, body=%wide.region_14.16_spmd.sunk | while | flops 1581060 | bytes 615053 | solution.py:22
  1162.4 17.1 %all-reduce = (f32[64,122]{1,0:T(8,128)S(1)}, f32[64,64]{1,0:T(8,128)S(1)}) all-reduce(f32[64,122]{1,0:T(8,128)S(1)} %fusion.21, f32[64,64]{1,0:T(8,128)S(1)} %fusion.39), channel_id=1, replica_groups=mesh['tgt'=64,'rep'=4] {'rep'}, use_global_device_ids=true, to_apply=%region_17.19 | all-reduce | flops 11904 | bytes 95232 | tf_op jit(solution)/shard_map/psum | solution.py:93
  1179.5 91.4 %while.67 = (s32[]{:T(128)}, f32[64,122]{1,0:T(8,128)S(1)}, f32[64,122]{1,0:T(8,128)S(1)}, f32[64,64]{1,0:T(8,128)S(1)}, s32[]{:T(128)}, /*index=5*/s32[]{:T(128)}, s32[]{:T(128)}, f32[1,1]{1,0:T(1,128)}) while((s32[]{:T(128)}, f32[64,122]{1,0:T(8,128)S(1)}, f32[64,122]{1,0:T(8,128)S(1)}, f32[64,64]{1,0:T(8,128)S(1)}, s32[]{:T(128)}, ...), condition=%wide.region_19.21_spmd, body=%wide.region_18.20_spmd.sunk | while | flops 94188 | bytes 37433 | solution.py:36
  (1041 shorter events, 343.4 us)
Async XLA Ops:
  13.6 27.5 %all-to-all-start.1 = ((s32[64,2,1]{1,2,0:T(1,128)}), s32[64,2,1]{1,2,0:T(1,128)S(1)}, u32[]{:S(2)}, u32[]{:S(2)}) async-start(s32[64,2,1]{1,2,0:T(1,128)} %bitcast.27), calls=%async_computation.1 | async-start | bytes 65536 | tf_op jit(solution)/shard_map/all_to_all | solution.py:67
  25.5 6.4 copy-start
  25.5 6.4 copy-start.3
  41.1 59.4 %all-to-all-start.3 = ((bf16[64,2,7808]{2,1,0:T(2,128)(2,1)}), bf16[64,2,7808]{2,1,0:T(2,128)(2,1)S(1)}, u32[]{:S(2)}, u32[]{:S(2)}) async-start(bf16[64,2,7808]{2,1,0:T(2,128)(2,1)} %all_to_all.45), calls=%async_computation.3 | async-start | bytes 3997696 | tf_op jit(solution)/shard_map/all_to_all | solution.py:66
  100.5 6.3 copy-start.2
  100.5 55.1 %all-to-all-start.2 = ((bf16[64,2,7808]{2,1,0:T(2,128)(2,1)}), bf16[64,2,7808]{2,1,0:T(2,128)(2,1)}, u32[]{:S(2)}, u32[]{:S(2)}) async-start(bf16[64,2,7808]{2,1,0:T(2,128)(2,1)} %all_to_all.42), calls=%async_computation.2 | async-start | bytes 3997696 | tf_op jit(solution)/shard_map/all_to_all | solution.py:65
  161.1 10.2 copy-start.4
  165.4 23.1 %all-to-all-start.4 = ((bf16[32,64,122]{2,0,1:T(8,128)(2,1)}), bf16[32,64,122]{2,0,1:T(8,128)(2,1)S(1)}, u32[]{:S(2)}, u32[]{:S(2)}) async-start(bf16[32,64,122]{2,0,1:T(8,128)(2,1)} %copy.22), calls=%async_computation.4 | async-start | bytes 1048576 | tf_op jit(solution)/shard_map/all_to_all | solution.py:76
  188.5 259.8 %all-to-all-start = ((f32[64,1,2048]{2,1,0:T(1,128)}), f32[64,1,2048]{2,1,0:T(1,128)S(1)}, u32[]{:S(2)}, u32[]{:S(2)}) async-start(f32[64,1,2048]{2,1,0:T(1,128)} %reshape.124), calls=%async_computation | async-start | bytes 1048576 | tf_op jit(solution)/shard_map/all_to_all | solution.py:78
  194.9 256.5 %all-reduce.5.cloned.1.call-start = ((), (), s32[]{:S(2)}) async-start(), calls=%async_computation.5 | async-start | bytes 1048576 | tf_op jit(solution)/shard_map/psum | solution.py:84
  196.1 783.5 %all-reduce.7.cloned.1.call-start = ((), (), s32[]{:S(2)}) async-start(), calls=%async_computation.6 | async-start | bytes 1048576 | tf_op jit(solution)/shard_map/psum | solution.py:84
  1270.9 0.6 copy-start.1
Sparse Core Ops, SparseCore 0:
  199.2 182.7 all-reduce.4
  733.2 176.5 all-reduce.6
